TPU v7x, 32 devices: a whole 2x2x4 slice. The times are simulated.
32 devices in a mesh: sta: 8 (over z, x), tpl: 4 (over y, core).
Axes of the slice: x: 2, y: 2, z: 4, core: 2. Of those that a mesh axis runs over, the one named last changes fastest.
Arguments:
- records: bfloat16 [256, 3, 4480], P(('sta', 'tpl')), may hold values from -6 to 6
- templates: bfloat16 [768, 10, 3, 200], P(('sta', 'tpl')), may hold values from -6 to 6
- pick_owner: int32 [768, 10], P(('sta', 'tpl')), may hold values from 0 to 31, all different within a row; in each aligned block of 24 rows (0 to 23, 24 to 47, ...) at most 12 rows name the same one
- pick_local: int32 [768, 10], P(('sta', 'tpl')), may hold values from 0 to 7
- moveout: int32 [768, 10], P(('sta', 'tpl')), may hold values from 0 to 127
- channel_mask: int32 [768, 10, 3], P(('sta', 'tpl')), may hold values 0 or 1
Outputs:
- detection: float32 [768, 4096], P(('sta', 'tpl'))
Inputs may be any that keep to these rules, and one draw needn't show every extreme that they name: `pick_owner`: each template names 10 different devices; among the templates of one device no device is named more than 12 times, and some device is named exactly 12 times.
All inputs are finite; a program needn't handle non-finite values. No bound on the sum of `channel_mask` on one device may be relied on, other than what follows from the above.
Results may differ from a plain program's by a relative error of at most 0.0029.
Values may be sent and summed in bfloat16 or wider, within the bound.
A program may use at most 128 MiB of HBM per device.

v0:
```python
import jax
import jax.numpy as jnp
from jax import lax
from jax.sharding import PartitionSpec as P

EPS = 1e-06


def toeplitz_rows(blocks, frame_len):
    group_size, channels, shape_len = blocks.shape
    padded = jnp.concatenate(
        [blocks, jnp.zeros((group_size, channels, frame_len + 1 - shape_len), blocks.dtype)], axis=2
    )
    repeated = jnp.broadcast_to(
        padded[:, :, None, :], (group_size, channels, 128, frame_len + 1)
    ).reshape(group_size, channels, 128 * (frame_len + 1))
    return repeated[:, :, : 128 * frame_len].reshape(group_size, channels, 128, frame_len)


def framed(records, frame_len):
    station_count, channels, record_len = records.shape
    pieces = records.reshape(station_count, channels, record_len // 128, 128)
    spread = frame_len // 128
    block_count = record_len // 128 - spread + 1
    return jnp.concatenate(
        [pieces[:, :, offset : offset + block_count, :] for offset in range(spread)], axis=3
    )


def on_device(records, templates, pick_owner, pick_local, moveout, channel_mask):
    devices = lax.axis_size(("sta", "tpl"))
    own_templates, pick_count, channels, shape_len = templates.shape
    frame_len = 128 + 128 * ((shape_len + 127) // 128)
    lag_count = records.shape[2] - frame_len
    lag_blocks = lag_count // 128
    capacity = max(2, (3 * own_templates * pick_count + 2 * devices - 1) // (2 * devices))
    pick_rows = own_templates * pick_count
    owners = pick_owner.reshape(pick_rows)
    onehot = (owners[:, None] == jnp.arange(devices, dtype=jnp.int32)[None, :]).astype(jnp.int32)
    before = jnp.cumsum(onehot, axis=0) - onehot
    position = owners * capacity + jnp.sum(before * onehot, axis=1)
    outbox = (
        jnp.zeros((devices * capacity, channels * shape_len), templates.dtype)
        .at[position]
        .set(templates.reshape(pick_rows, channels * shape_len))
    )
    details = jnp.concatenate(
        [
            pick_local.reshape(pick_rows, 1),
            channel_mask.reshape(pick_rows, channels),
            moveout.reshape(pick_rows, 1),
        ],
        axis=1,
    )
    labels = jnp.zeros((devices * capacity, channels + 2), jnp.int32).at[position].set(details)
    arrived, arrived_marks = (
        lax.all_to_all(
            outbox.reshape(devices, capacity, channels * shape_len),
            ("sta", "tpl"),
            split_axis=0,
            concat_axis=0,
            tiled=True,
        ),
        lax.all_to_all(
            labels.reshape(devices, capacity, channels + 2),
            ("sta", "tpl"),
            split_axis=0,
            concat_axis=0,
            tiled=True,
        ),
    )
    slot_count = devices * capacity
    frames = framed(records, frame_len)
    squares = jnp.square(frames.astype(jnp.float32))
    offsets = (
        jnp.arange(frame_len, dtype=jnp.int32)[:, None] - jnp.arange(128, dtype=jnp.int32)[None, :]
    )
    band = ((offsets >= 0) & (offsets < shape_len)).astype(jnp.float32)
    energy = jnp.einsum("scbm,mj->scbj", squares, band, precision=lax.Precision.HIGHEST)
    group_size = 64
    source_index = jnp.arange(256, dtype=jnp.int32)[:, None]
    target_index = jnp.arange(128, dtype=jnp.int32)[None, :]

    def correlate(pieces):
        shapes, slot_marks = pieces
        stations = slot_marks[:, 0]
        toeplitz = toeplitz_rows(shapes, frame_len)
        windows = frames[stations]
        numerator = jnp.einsum(
            "gcbm,gcjm->gcbj", windows, toeplitz, preferred_element_type=jnp.float32
        )
        template_power = jnp.sum(jnp.square(shapes.astype(jnp.float32)), axis=2)
        scaled = numerator * lax.rsqrt(template_power[:, :, None, None] * energy[stations] + EPS)
        weights = slot_marks[:, 1 : 1 + channels].astype(jnp.float32)
        traces = jnp.sum(weights[:, :, None, None] * scaled, axis=1).astype(jnp.bfloat16)
        paired = jnp.concatenate(
            [traces[:, :lag_blocks, :], traces[:, 1 : lag_blocks + 1, :]], axis=2
        )
        shifts = slot_marks[:, channels + 1]
        selector = (
            source_index[None, :, :] == target_index[None, :, :] + shifts[:, None, None]
        ).astype(jnp.bfloat16)
        aligned = jnp.einsum("gbi,gij->gbj", paired, selector, preferred_element_type=jnp.float32)
        return aligned.astype(jnp.bfloat16).reshape(group_size, lag_count)

    outgoing = lax.map(
        correlate,
        (
            arrived.reshape(slot_count // group_size, group_size, channels, shape_len),
            arrived_marks.reshape(slot_count // group_size, group_size, channels + 2),
        ),
    )
    returned = lax.all_to_all(
        outgoing.reshape(devices, capacity, lag_count),
        ("sta", "tpl"),
        split_axis=0,
        concat_axis=0,
        tiled=True,
    )
    picked = returned.reshape(slot_count, lag_count)[position].astype(jnp.float32)
    stacked = jnp.sum(picked.reshape(own_templates, pick_count, lag_count), axis=1)
    levels = jnp.sqrt(jnp.mean(stacked * stacked, axis=1, keepdims=True) + EPS)
    return stacked / levels


def solution(mesh):
    return jax.shard_map(
        on_device,
        mesh=mesh,
        in_specs=(
            P(("sta", "tpl"), None, None),
            P(("sta", "tpl"), None, None, None),
            P(("sta", "tpl"), None),
            P(("sta", "tpl"), None),
            P(("sta", "tpl"), None),
            P(("sta", "tpl"), None, None),
        ),
        out_specs=P(("sta", "tpl"), None),
        check_vma=False,
    )
```

profile of v0, /device:TPU:0, one launch (start us, length us, event | category | flops | bytes accessed | tf_op | source)
XLA Modules:
  0.0 657.1 jit_solution(1735345931388154163)
XLA Ops:
  7.7 7.3 %all-to-all-start = ((s32[32,12,5]{1,2,0:T(8,128)}), s32[32,12,5]{1,2,0:T(8,128)S(1)}, u32[]{:S(2)}, u32[]{:S(2)}) async-start(s32[32,12,5]{1,2,0:T(8,128)} %copy.70), calls=%async_computation | async-start | bytes 262144 | tf_op jit(solution)/shard_map/all_to_all | solution.py:64
  27.5 16.3 %all-to-all-done.1 = bf16[32,12,600]{2,1,0:T(8,128)(2,1)S(1)} async-done(((bf16[32,12,600]{2,1,0:T(8,128)(2,1)}), bf16[32,12,600]{2,1,0:T(8,128)(2,1)S(1)}, u32[]{:S(2)}, u32[]{:S(2)}) %all-to-all-start.1) | async-done | bytes 460832 | tf_op jit(solution)/shard_map/all_to_all | solution.py:57
  44.5 492.4 %while.11 = (s32[]{:T(128)}, bf16[6,64,4096]{2,1,0:T(8,128)(2,1)}, s32[6,64,5]{1,0,2:T(8,128)S(1)}, bf16[8,3,33,384]{3,2,1,0:T(8,128)(2,1)S(1)}, bf16[6,64,3,200...) while((s32[]{:T(128)}, bf16[6,64,4096]{2,1,0:T(8,128)(2,1)}, ...), condition=%wide.region_8.9_spmd.clone, body=%wide.region_5.8_spmd.clone.sunk | while | flops 765437632 | bytes 201265280 | solution.py:106
  51.3 8.4 %broadcast_in_dim.41 = bf16[64,3,128,385]{3,2,0,1:T(8,128)(2,1)} broadcast(bf16[64,3,385]{2,0,1:T(8,128)(2,1)S(1)} %concatenate.17), dimensions={0,1,3} | broadcast | bytes 19071360 | tf_op jit(solution)/shard_map/while/body/eval_jaxpr/broadcast_in_dim | solution.py:14
  59.7 35.9 %reshape.205 = bf16[64,3,49280]{2,0,1:T(8,128)(2,1)} reshape(bf16[64,3,128,385]{3,2,0,1:T(8,128)(2,1)} %broadcast_in_dim.41) | data formatting | bytes 37847040 | tf_op jit(solution)/shard_map/while/body/eval_jaxpr/reshape | solution.py:16
  102.0 7.0 %copy.104 = bf16[24,8,128,384]{3,2,1,0:T(8,128)(2,1)} copy(bf16[24,8,128,384]{3,1,2,0:T(8,128)(2,1)S(1)} %bitcast.59) | data formatting | bytes 37748736 | tf_op jit(solution)/shard_map/while
  109.2 14.0 %multiply_reduce_fusion.6 = bf16[64,33,128]{2,1,0:T(8,128)(2,1)S(1)} fusion(f32[64,3,33,128]{3,2,1,0:T(8,128)} %gather_fusion, f32[64,3]{1,0:T(8,128)S(1)} %copy.102, f32[64,3]{1,0:T(8,128)S(1)} %copy.103, bf16[64,3,33,384]{3,2,1,0:T(8,128)(2,1)} %gather_fusion.1, bf16[64,3,128,384]{3,2,0,1:T(8,128)(2,1)} %bitcast.60), kind=kOutput, calls=%fused_computation.12.clone.1 | convolution fusion | flops 626638848 | bytes 27526656 | tf_op jit(solution)/shard_map/while/body/eval_jaxpr/gcbm,gcjm->gcbj/dot_general | solution.py:89
  133.3 8.4 %broadcast_in_dim.41 = bf16[64,3,128,385]{3,2,0,1:T(8,128)(2,1)} broadcast(bf16[64,3,385]{2,0,1:T(8,128)(2,1)S(1)} %concatenate.17), dimensions={0,1,3} | broadcast | bytes 19071360 | tf_op jit(solution)/shard_map/while/body/eval_jaxpr/broadcast_in_dim | solution.py:14
  141.8 35.9 %reshape.205 = bf16[64,3,49280]{2,0,1:T(8,128)(2,1)} reshape(bf16[64,3,128,385]{3,2,0,1:T(8,128)(2,1)} %broadcast_in_dim.41) | data formatting | bytes 37847040 | tf_op jit(solution)/shard_map/while/body/eval_jaxpr/reshape | solution.py:16
  191.3 14.0 %multiply_reduce_fusion.6 = bf16[64,33,128]{2,1,0:T(8,128)(2,1)S(1)} fusion(f32[64,3,33,128]{3,2,1,0:T(8,128)} %gather_fusion, f32[64,3]{1,0:T(8,128)S(1)} %copy.102, f32[64,3]{1,0:T(8,128)S(1)} %copy.103, bf16[64,3,33,384]{3,2,1,0:T(8,128)(2,1)} %gather_fusion.1, bf16[64,3,128,384]{3,2,0,1:T(8,128)(2,1)} %bitcast.60), kind=kOutput, calls=%fused_computation.12.clone.1 | convolution fusion | flops 626638848 | bytes 27526656 | tf_op jit(solution)/shard_map/while/body/eval_jaxpr/gcbm,gcjm->gcbj/dot_general | solution.py:89
  215.4 8.4 %broadcast_in_dim.41 = bf16[64,3,128,385]{3,2,0,1:T(8,128)(2,1)} broadcast(bf16[64,3,385]{2,0,1:T(8,128)(2,1)S(1)} %concatenate.17), dimensions={0,1,3} | broadcast | bytes 19071360 | tf_op jit(solution)/shard_map/while/body/eval_jaxpr/broadcast_in_dim | solution.py:14
  223.8 35.9 %reshape.205 = bf16[64,3,49280]{2,0,1:T(8,128)(2,1)} reshape(bf16[64,3,128,385]{3,2,0,1:T(8,128)(2,1)} %broadcast_in_dim.41) | data formatting | bytes 37847040 | tf_op jit(solution)/shard_map/while/body/eval_jaxpr/reshape | solution.py:16
  273.4 14.0 %multiply_reduce_fusion.6 = bf16[64,33,128]{2,1,0:T(8,128)(2,1)S(1)} fusion(f32[64,3,33,128]{3,2,1,0:T(8,128)} %gather_fusion, f32[64,3]{1,0:T(8,128)S(1)} %copy.102, f32[64,3]{1,0:T(8,128)S(1)} %copy.103, bf16[64,3,33,384]{3,2,1,0:T(8,128)(2,1)} %gather_fusion.1, bf16[64,3,128,384]{3,2,0,1:T(8,128)(2,1)} %bitcast.60), kind=kOutput, calls=%fused_computation.12.clone.1 | convolution fusion | flops 626638848 | bytes 27526656 | tf_op jit(solution)/shard_map/while/body/eval_jaxpr/gcbm,gcjm->gcbj/dot_general | solution.py:89
  297.5 8.4 %broadcast_in_dim.41 = bf16[64,3,128,385]{3,2,0,1:T(8,128)(2,1)} broadcast(bf16[64,3,385]{2,0,1:T(8,128)(2,1)S(1)} %concatenate.17), dimensions={0,1,3} | broadcast | bytes 19071360 | tf_op jit(solution)/shard_map/while/body/eval_jaxpr/broadcast_in_dim | solution.py:14
  305.9 35.9 %reshape.205 = bf16[64,3,49280]{2,0,1:T(8,128)(2,1)} reshape(bf16[64,3,128,385]{3,2,0,1:T(8,128)(2,1)} %broadcast_in_dim.41) | data formatting | bytes 37847040 | tf_op jit(solution)/shard_map/while/body/eval_jaxpr/reshape | solution.py:16
  348.2 7.0 %copy.104 = bf16[24,8,128,384]{3,2,1,0:T(8,128)(2,1)} copy(bf16[24,8,128,384]{3,1,2,0:T(8,128)(2,1)S(1)} %bitcast.59) | data formatting | bytes 37748736 | tf_op jit(solution)/shard_map/while
  355.4 14.0 %multiply_reduce_fusion.6 = bf16[64,33,128]{2,1,0:T(8,128)(2,1)S(1)} fusion(f32[64,3,33,128]{3,2,1,0:T(8,128)} %gather_fusion, f32[64,3]{1,0:T(8,128)S(1)} %copy.102, f32[64,3]{1,0:T(8,128)S(1)} %copy.103, bf16[64,3,33,384]{3,2,1,0:T(8,128)(2,1)} %gather_fusion.1, bf16[64,3,128,384]{3,2,0,1:T(8,128)(2,1)} %bitcast.60), kind=kOutput, calls=%fused_computation.12.clone.1 | convolution fusion | flops 626638848 | bytes 27526656 | tf_op jit(solution)/shard_map/while/body/eval_jaxpr/gcbm,gcjm->gcbj/dot_general | solution.py:89
  379.5 8.4 %broadcast_in_dim.41 = bf16[64,3,128,385]{3,2,0,1:T(8,128)(2,1)} broadcast(bf16[64,3,385]{2,0,1:T(8,128)(2,1)S(1)} %concatenate.17), dimensions={0,1,3} | broadcast | bytes 19071360 | tf_op jit(solution)/shard_map/while/body/eval_jaxpr/broadcast_in_dim | solution.py:14
  387.9 35.9 %reshape.205 = bf16[64,3,49280]{2,0,1:T(8,128)(2,1)} reshape(bf16[64,3,128,385]{3,2,0,1:T(8,128)(2,1)} %broadcast_in_dim.41) | data formatting | bytes 37847040 | tf_op jit(solution)/shard_map/while/body/eval_jaxpr/reshape | solution.py:16
  437.5 14.0 %multiply_reduce_fusion.6 = bf16[64,33,128]{2,1,0:T(8,128)(2,1)S(1)} fusion(f32[64,3,33,128]{3,2,1,0:T(8,128)} %gather_fusion, f32[64,3]{1,0:T(8,128)S(1)} %copy.102, f32[64,3]{1,0:T(8,128)S(1)} %copy.103, bf16[64,3,33,384]{3,2,1,0:T(8,128)(2,1)} %gather_fusion.1, bf16[64,3,128,384]{3,2,0,1:T(8,128)(2,1)} %bitcast.60), kind=kOutput, calls=%fused_computation.12.clone.1 | convolution fusion | flops 626638848 | bytes 27526656 | tf_op jit(solution)/shard_map/while/body/eval_jaxpr/gcbm,gcjm->gcbj/dot_general | solution.py:89
  461.5 8.4 %broadcast_in_dim.41 = bf16[64,3,128,385]{3,2,0,1:T(8,128)(2,1)} broadcast(bf16[64,3,385]{2,0,1:T(8,128)(2,1)S(1)} %concatenate.17), dimensions={0,1,3} | broadcast | bytes 19071360 | tf_op jit(solution)/shard_map/while/body/eval_jaxpr/broadcast_in_dim | solution.py:14
  470.0 35.9 %reshape.205 = bf16[64,3,49280]{2,0,1:T(8,128)(2,1)} reshape(bf16[64,3,128,385]{3,2,0,1:T(8,128)(2,1)} %broadcast_in_dim.41) | data formatting | bytes 37847040 | tf_op jit(solution)/shard_map/while/body/eval_jaxpr/reshape | solution.py:16
  519.5 14.0 %multiply_reduce_fusion.6 = bf16[64,33,128]{2,1,0:T(8,128)(2,1)S(1)} fusion(f32[64,3,33,128]{3,2,1,0:T(8,128)} %gather_fusion, f32[64,3]{1,0:T(8,128)S(1)} %copy.102, f32[64,3]{1,0:T(8,128)S(1)} %copy.103, bf16[64,3,33,384]{3,2,1,0:T(8,128)(2,1)} %gather_fusion.1, bf16[64,3,128,384]{3,2,0,1:T(8,128)(2,1)} %bitcast.60), kind=kOutput, calls=%fused_computation.12.clone.1 | convolution fusion | flops 626638848 | bytes 27526656 | tf_op jit(solution)/shard_map/while/body/eval_jaxpr/gcbm,gcjm->gcbj/dot_general | solution.py:89
  546.3 94.4 %all-to-all-done.2 = bf16[32,12,4096]{2,1,0:T(8,128)(2,1)} async-done(((bf16[32,12,4096]{2,1,0:T(8,128)(2,1)}), bf16[32,12,4096]{2,1,0:T(8,128)(2,1)}, u32[]{:S(2)}, u32[]{:S(2)}) %all-to-all-start.2) | async-done | bytes 3145760 | tf_op jit(solution)/shard_map/all_to_all | solution.py:113
  (170 shorter events, 174.3 us)
Async XLA Ops:
  0.0 26.1 %copy-start = (bf16[8,3,4480]{2,0,1:T(8,128)(2,1)S(1)}, bf16[8,3,4480]{2,0,1:T(8,128)(2,1)}, u32[]{:S(2)}) copy-start(bf16[8,3,4480]{2,0,1:T(8,128)(2,1)} %param.8) | copy-start | bytes 645124
  5.6 20.6 %copy-start.1 = (s32[240,1]{0,1:T(1,128)}, s32[240,1]{0,1:T(1,128)S(1)}, u32[]{:S(2)}) copy-start(s32[240,1]{0,1:T(1,128)S(1)} %compare_select_fusion.1) | copy-start | bytes 2884
  7.7 15.5 %all-to-all-start = ((s32[32,12,5]{1,2,0:T(8,128)}), s32[32,12,5]{1,2,0:T(8,128)S(1)}, u32[]{:S(2)}, u32[]{:S(2)}) async-start(s32[32,12,5]{1,2,0:T(8,128)} %copy.70), calls=%async_computation | async-start | bytes 262144 | tf_op jit(solution)/shard_map/all_to_all | solution.py:64
  23.3 20.5 %all-to-all-start.1 = ((bf16[32,12,600]{2,1,0:T(8,128)(2,1)}), bf16[32,12,600]{2,1,0:T(8,128)(2,1)S(1)}, u32[]{:S(2)}, u32[]{:S(2)}) async-start(bf16[32,12,600]{2,1,0:T(8,128)(2,1)} %reshape.137), calls=%async_computation.1 | async-start | bytes 1310720 | tf_op jit(solution)/shard_map/all_to_all | solution.py:57
  95.6 6.4 slice-start
  177.7 6.4 slice-start
  259.8 6.4 slice-start
  341.8 6.4 slice-start
  423.9 6.4 slice-start
  505.9 6.4 slice-start
  542.3 3.9 copy-start.2
  542.3 98.3 %all-to-all-start.2 = ((bf16[32,12,4096]{2,1,0:T(8,128)(2,1)}), bf16[32,12,4096]{2,1,0:T(8,128)(2,1)}, u32[]{:S(2)}, u32[]{:S(2)}) async-start(bf16[32,12,4096]{2,1,0:T(8,128)(2,1)} %reshape.139), calls=%async_computation.2 | async-start | bytes 8388608 | tf_op jit(solution)/shard_map/all_to_all | solution.py:113
where the time goes:
time: 663 us; the launch traced here: 657 us
  local copies, waits for them, and re-layouts  424 us (64%)
  waiting for transfers between devices  115 us (17%)
  matrix products  95.9 us (14%)
  starting transfers between devices  14 us (2%)
  other arithmetic  7.77 us (1%)
    reshape x6, local copies, waits for them, and re-layouts, toeplitz_rows(): repeated = jnp.broadcast_to(padded[:, :, None, :], (group_size, channels,...  216 us
    all_to_all x1, waiting for transfers between devices, on_device(): lax.all_to_all(outgoing.reshape(devices, capacity, lag_count), ('sta', 't...  94.4 us
    dot_general x6, matrix products, correlate(): jnp.einsum('gcbm,gcjm->gcbj', windows, toeplitz, preferred_element_type=j...  83.8 us
    broadcast_in_dim x6, local copies, waits for them, and re-layouts, toeplitz_rows(): jnp.broadcast_to(padded[:, :, None, :], (group_size, channels, 128, frame...  50.7 us
    while x6, local copies, waits for them, and re-layouts  42.3 us
    slice x12, local copies, waits for them, and re-layouts, toeplitz_rows(): repeated[:, :, :128 * frame_len]  38.2 us
    gather x6, local copies, waits for them, and re-layouts, correlate(): windows = frames[stations]  23.5 us
    all_to_all x1, waiting for transfers between devices, on_device(): lax.all_to_all(outbox.reshape(devices, capacity, channels * shape_len), (...  16.3 us
  transfers between devices with their start and end apart: 3, of which 3 were waited for; matrix products, arithmetic and copies ran while one was open for 1% of the time, Pallas kernels for 0%

commit v1 on v0

v1 whole, which is shorter than its diff:
```python
import functools

import jax
import jax.numpy as jnp
from jax import lax
from jax.experimental import pallas as pl
from jax.experimental.pallas import tpu as pltpu
from jax.sharding import PartitionSpec as P

EPS = 1e-06
LANES = 128


def toeplitz(row):
    base = pltpu.roll(
        jnp.broadcast_to(row, (16, 256)), 0, axis=1, stride=1, stride_axis=0
    ).astype(jnp.bfloat16)
    zeros = jnp.zeros((16, LANES), jnp.bfloat16)
    wide = jnp.concatenate([base, zeros], axis=1)
    strips = [wide]
    for step in range(1, 8):
        strips.append(
            jnp.concatenate([zeros[:, : 16 * step], wide[:, : 384 - 16 * step]], axis=1)
        )
    return jnp.concatenate(strips, axis=0)


def stack_kernel(picks, channels, blocks, station, shift, power, mask, band_ref, shapes_ref, *rest):
    record_refs, out_ref, wide_ref, squares_ref, energy_ref = rest[:picks], *rest[picks:]
    pieces = record_refs[0].shape[1] // channels
    rows = squares_ref.shape[0] // (picks * channels)
    template = pl.program_id(0)
    shapes = shapes_ref[0].astype(jnp.float32)
    for pick in range(picks):
        wide_ref[pick, : channels * pieces] = record_refs[pick][0].astype(jnp.float32)
    windows = []
    for pick in range(picks):
        for channel in range(channels):
            parts = [
                wide_ref[pick, channel * pieces + k : channel * pieces + k + rows]
                for k in range(3)
            ]
            windows.append(jnp.concatenate([part.astype(jnp.bfloat16) for part in parts], axis=1))
            item = pick * channels + channel
            squares_ref[item * rows : (item + 1) * rows] = jnp.concatenate(
                [(part * part).astype(jnp.bfloat16) for part in parts], axis=1
            )
    energy_ref[...] = jnp.dot(
        squares_ref[...], band_ref[...], preferred_element_type=jnp.float32
    )
    lane = lax.broadcasted_iota(jnp.int32, (blocks, LANES), 1)
    total = jnp.zeros((blocks, LANES), jnp.float32)
    for pick in range(picks):
        trace = jnp.zeros((rows, LANES), jnp.float32)
        for channel in range(channels):
            item = pick * channels + channel
            at = template * (picks * channels) + item
            correlation = lax.dot_general(
                windows[item],
                toeplitz(shapes[item : item + 1]),
                (((1,), (1,)), ((), ())),
                preferred_element_type=jnp.float32,
            )
            scale = lax.rsqrt(power[at] * energy_ref[item * rows : (item + 1) * rows] + EPS)
            trace = trace + mask[at] * (correlation * scale)
        trace = trace.astype(jnp.bfloat16).astype(jnp.float32)
        moved = shift[template * picks + pick]
        turned = pltpu.roll(trace, lax.rem(LANES - moved, LANES), axis=1)
        total = total + jnp.where(
            lane < LANES - moved, turned[:blocks], turned[1 : blocks + 1]
        )
    mean = jnp.sum(total * total) / (blocks * LANES)
    out_ref[0] = total * lax.rsqrt(jnp.full((blocks, LANES), mean + EPS, jnp.float32))


def on_device(records, templates, pick_owner, pick_local, moveout, channel_mask):
    own_stations, channels, record_len = records.shape
    own_templates, picks, _, shape_len = templates.shape
    pieces = record_len // LANES
    frame_len = 3 * LANES
    blocks = (record_len - frame_len) // LANES
    rows = -(-(blocks + 1) // 8) * 8
    everywhere = lax.all_gather(
        records.reshape(own_stations, channels * pieces, LANES), ("sta", "tpl"), axis=0, tiled=True
    )
    station = (pick_owner * own_stations + pick_local).reshape(-1)
    power = jnp.sum(jnp.square(templates.astype(jnp.float32)), axis=3).reshape(-1)
    mask = channel_mask.astype(jnp.float32).reshape(-1)
    items = picks * channels
    shapes = jnp.pad(
        templates.reshape(own_templates, items, shape_len),
        ((0, 0), (0, -items % 16), (0, 2 * LANES - shape_len)),
    )
    offsets = (
        jnp.arange(frame_len, dtype=jnp.int32)[:, None] - jnp.arange(LANES, dtype=jnp.int32)[None, :]
    )
    band = ((offsets >= 0) & (offsets < shape_len)).astype(jnp.bfloat16)

    def record_spec(pick):
        return pl.BlockSpec(
            (1, channels * pieces, LANES),
            lambda t, station, shift, power, mask: (station[t * picks + pick], 0, 0),
        )

    wide_rows = -(-((channels - 1) * pieces + 2 + rows) // 8) * 8
    stacked = pl.pallas_call(
        functools.partial(stack_kernel, picks, channels, blocks),
        grid_spec=pltpu.PrefetchScalarGridSpec(
            num_scalar_prefetch=4,
            grid=(own_templates,),
            in_specs=[
                pl.BlockSpec((frame_len, LANES), lambda t, *_: (0, 0)),
                pl.BlockSpec((1,) + shapes.shape[1:], lambda t, *_: (t, 0, 0)),
            ]
            + [record_spec(pick) for pick in range(picks)],
            out_specs=pl.BlockSpec((1, blocks, LANES), lambda t, *_: (t, 0, 0)),
            scratch_shapes=[
                pltpu.VMEM((picks, wide_rows, LANES), jnp.float32),
                pltpu.VMEM((items * rows, frame_len), jnp.bfloat16),
                pltpu.VMEM((items * rows, LANES), jnp.float32),
            ],
        ),
        out_shape=jax.ShapeDtypeStruct((own_templates, blocks, LANES), jnp.float32),
        compiler_params=pltpu.CompilerParams(vmem_limit_bytes=48 * 1024 * 1024),
    )(station, moveout.reshape(-1), power, mask, band, shapes, *([everywhere] * picks))
    return stacked.reshape(own_templates, blocks * LANES)


def solution(mesh):
    return jax.shard_map(
        on_device,
        mesh=mesh,
        in_specs=(
            P(("sta", "tpl"), None, None),
            P(("sta", "tpl"), None, None, None),
            P(("sta", "tpl"), None),
            P(("sta", "tpl"), None),
            P(("sta", "tpl"), None),
            P(("sta", "tpl"), None, None),
        ),
        out_specs=P(("sta", "tpl"), None),
        check_vma=False,
    )
```

time: 663 us -> 180 us (0.27)
  local copies, waits for them, and re-layouts: 424 us -> 14.3 us
  matrix products: 95.9 us -> 0 us
  Pallas kernels: 0 us -> 65.9 us
  waiting for transfers between devices: 115 us -> 83.6 us
  starting transfers between devices: 14 us -> 0.01 us
  between operations: 0.26 us -> 13.5 us
    reshape x17 -> x5, local copies, waits for them, and re-layouts: 228 us -> 1.66 us  [the longest x1 1.07 us: on_device(): templates.reshape(own_templates, items, shape_len)]
    all_to_all x3 -> x0, waiting for transfers between devices: 115 us -> none  [the longest x1 94.4 us: on_device(): lax.all_to_all(outgoing.reshape(devices, capacity, lag_count), ('sta', 't...]
    dot_general x13 -> x0, matrix products: 95.9 us -> none  [the longest x6 83.8 us: correlate(): jnp.einsum('gcbm,gcjm->gcbj', windows, toeplitz, preferred_element_type=j...]
    all_gather x0 -> x1, waiting for transfers between devices: none -> 82.9 us  [on_device(): lax.all_gather(records.reshape(own_stations, channels * pieces, LANES), (...]
    pallas_call x0 -> x1, Pallas kernels: none -> 65.9 us  [on_device(): pl.pallas_call(functools.partial(stack_kernel, picks, channels, blocks),...]
    broadcast_in_dim x12 -> x0, local copies, waits for them, and re-layouts: 52 us -> none  [the longest x6 50.7 us: toeplitz_rows(): jnp.broadcast_to(padded[:, :, None, :], (group_size, channels, 128, frame...]
    gather x13 -> x0, local copies, waits for them, and re-layouts: 42.6 us -> none  [the longest x6 23.5 us: correlate(): windows = frames[stations]]
    while x6 -> x0, local copies, waits for them, and re-layouts: 42.3 us -> none
  transfers between devices with their start and end apart: 3 -> 1, of which waited for: 3 -> 1; matrix products, arithmetic and copies ran while one was open for 1% -> 3% of each run, Pallas kernels for 0% -> 0%
where the time goes in v1:
time: 180 us
  waiting for transfers between devices  83.6 us (46%)
  Pallas kernels  65.9 us (37%)
  local copies, waits for them, and re-layouts  14.3 us (8%)
  between operations  13.5 us (8%)
  other arithmetic  2.66 us (1%)
    all_gather x1, waiting for transfers between devices, on_device(): lax.all_gather(records.reshape(own_stations, channels * pieces, LANES), (...  82.9 us
    pallas_call x1, Pallas kernels, on_device(): pl.pallas_call(functools.partial(stack_kernel, picks, channels, blocks),...  65.9 us
    all_gather x1, local copies, waits for them, and re-layouts, on_device(): lax.all_gather(records.reshape(own_stations, channels * pieces, LANES), (...  10.4 us
  transfers between devices with their start and end apart: 1, of which 1 were waited for; matrix products, arithmetic and copies ran while one was open for 3% of the time, Pallas kernels for 0%

profile of v1, /device:TPU:0, one launch (start us, length us, event | category | flops | bytes accessed | tf_op | source)
XLA Modules:
  0.0 180.0 jit_solution(3907286820732068344)
XLA Ops:
  6.5 0.0 all-gather.2.cloned.1.call-start
  6.5 0.7 all-gather.2.cloned.1.call-update
  7.3 1.1 copy.36
  8.3 0.7 copy_convert_fusion
  9.1 0.2 copy.35
  9.3 0.2 reshape.24.mask
  9.5 1.2 multiply_reduce_fusion
  10.6 0.2 copy.33
  10.8 0.2 reshape.23.power
  11.0 0.7 multiply_add_fusion
  11.7 0.1 copy.31
  11.8 0.1 reshape.21.station
  11.9 0.8 copy.32
  12.7 0.1 reshape.22.shift
  12.8 0.1 pad.4.shapes_ref
  12.9 82.9 %all-gather.2.cloned.1.call-done = bf16[256,105,128]{2,0,1:T(8,128)(2,1)} async-done(((bf16[8,105,128]{2,0,1:T(8,128)(2,1)}), bf16[256,105,128]{2,0,1:T(8,128)(2,1)}) %all-gather.2.cloned.1.call-update) | async-done | bytes 6881296 | tf_op jit(solution)/shard_map/all_gather | solution.py:83
  95.8 10.4 %copy.39.rest_0_.rest_1_.rest_2_.rest_3_.rest_4_.rest_5_.rest_6_.rest_7_.rest_8_.rest_9_ = bf16[256,105,128]{2,1,0:T(8,128)(2,1)} copy(bf16[256,105,128]{2,0,1:T(8,128)(2,1)} %all-gather.2.cloned.1.call-done) | data formatting | bytes 13762560 | tf_op jit(solution)/shard_map/all_gather | solution.py:83
  106.2 65.9 %shard_map.64 = f32[24,32,128]{2,1,0:T(8,128)S(1)} custom-call(s32[240]{0:T(256)S(1)} %reshape.21.station, s32[240]{0:T(256)S(1)} %reshape.22.shift, f32[720]{0:T(1024)S(1)} %reshape.23.power, f32[720]{0:T(1024)S(1)} %reshape.24.mask, bf16[384,128]{1,0:T(8,128)(2,1)S(1)} %fusion.3.band_ref, bf16[24,32,256]{2,1,0:T(8,128)(2,1)S(1)} %pad.4.shapes_ref, ...), custom_call_target="tpu_custom_call" | custom-call | tf_op jit(solution)/shard_map/pallas_call | solution.py:106
  172.1 1.0 copy.52
  (1 shorter events, 0.0 us)
Async XLA Ops:
  6.5 89.3 %all-gather.2.cloned.1.call-start = ((), (), s32[]{:S(2)}) async-start(), calls=%async_computation | async-start | bytes 7096320 | tf_op jit(solution)/shard_map/all_gather | solution.py:83
Sparse Core Ops, SparseCore 0:
  10.2 85.5 all-gather.1

commit v2 on v1

v2 whole, which is shorter than its diff:
```python
import functools

import jax
import jax.numpy as jnp
from jax import lax
from jax.experimental import pallas as pl
from jax.experimental.pallas import tpu as pltpu
from jax.sharding import PartitionSpec as P

EPS = 1e-06
LANES = 128
MESH = pl.DeviceIdType.MESH


def toeplitz(row):
    base = pltpu.roll(
        jnp.broadcast_to(row, (16, 256)), 0, axis=1, stride=1, stride_axis=0
    ).astype(jnp.bfloat16)
    zeros = jnp.zeros((16, LANES), jnp.bfloat16)
    wide = jnp.concatenate([base, zeros], axis=1)
    strips = [wide]
    for step in range(1, 8):
        strips.append(
            jnp.concatenate([zeros[:, : 16 * step], wide[:, : 384 - 16 * step]], axis=1)
        )
    return jnp.concatenate(strips, axis=0)


def stack_kernel(picks, channels, pieces, station, shift, power, mask, band_ref, shapes_ref, *rest):
    record_refs, out_ref, wide_ref, squares_ref, energy_ref = rest[:picks], *rest[picks:]
    blocks = out_ref.shape[1]
    held = record_refs[0].shape[1]
    template = pl.program_id(0)
    shapes = shapes_ref[0].astype(jnp.float32)
    lane = lax.broadcasted_iota(jnp.int32, (held, LANES), 1)
    windows = []
    for pick in range(picks):
        moved = shift[template * picks + pick]
        wide_ref[pick, :held] = pltpu.roll(
            record_refs[pick][0].astype(jnp.float32), lax.rem(LANES - moved, LANES), axis=1
        )
        wide_ref[pick, :held] = jnp.where(
            lane < LANES - moved, wide_ref[pick, :held], wide_ref[pick, 1 : held + 1]
        )
        for channel in range(channels):
            first = channel * pieces
            window = jnp.concatenate(
                [
                    wide_ref[pick, first + k : first + k + blocks].astype(jnp.bfloat16)
                    for k in range(3)
                ],
                axis=1,
            )
            windows.append(window)
            item = pick * channels + channel
            squares_ref[item * blocks : (item + 1) * blocks] = window * window
    energy_ref[...] = jnp.dot(
        squares_ref[...], band_ref[...], preferred_element_type=jnp.float32
    )
    total = jnp.zeros((blocks, LANES), jnp.float32)
    for pick in range(picks):
        trace = jnp.zeros((blocks, LANES), jnp.float32)
        for channel in range(channels):
            item = pick * channels + channel
            at = template * (picks * channels) + item
            correlation = lax.dot_general(
                windows[item],
                toeplitz(shapes[item : item + 1]),
                (((1,), (1,)), ((), ())),
                preferred_element_type=jnp.float32,
            )
            scale = lax.rsqrt(power[at] * energy_ref[item * blocks : (item + 1) * blocks] + EPS)
            trace = trace + mask[at] * (correlation * scale)
        total = total + trace.astype(jnp.bfloat16).astype(jnp.float32)
    mean = jnp.sum(total * total) / (blocks * LANES)
    out_ref[0] = total * lax.rsqrt(jnp.full((blocks, LANES), mean + EPS, jnp.float32))


def gather_kernel(mine_ref, all_ref, local_sem, send_sem, recv_sem):
    stations = mine_ref.shape[0]
    sta, tpl = lax.axis_index("sta"), lax.axis_index("tpl")
    z, x, y, core = sta // 2, sta % 2, tpl // 2, tpl % 2
    first_x, first_y = x + (1 - core) * (1 - 2 * x), y + core * (1 - 2 * y)
    second_x, second_y = x + core * (1 - 2 * x), y + (1 - core) * (1 - 2 * y)
    heights = [z, z + 1 - 2 * (z % 2), (z + 2) % 4, 3 - z]
    first = (z * 2 + first_x, first_y * 2 + core)
    second = (z * 2 + second_x, second_y * 2 + core)
    sibling = (sta, y * 2 + 1 - core)
    partners = [(height * 2 + x, tpl) for height in heights[1:]] + [first, second, sibling]

    barrier = pltpu.get_barrier_semaphore()
    for partner in partners:
        pl.semaphore_signal(barrier, inc=1, device_id=partner, device_id_type=MESH)
    pl.semaphore_wait(barrier, len(partners))

    def number(height, at_x, at_y, at_core):
        return (height * 2 + at_x) * 4 + at_y * 2 + at_core

    def block(shard):
        return all_ref.at[pl.ds(shard * stations, stations)]

    started = []

    def send(source, shard, partner):
        copy = pltpu.make_async_remote_copy(
            src_ref=source,
            dst_ref=block(shard),
            send_sem=send_sem.at[len(started)],
            recv_sem=recv_sem.at[shard],
            device_id=partner,
            device_id_type=MESH,
        )
        copy.start()
        started.append(copy)

    def arrive(shard):
        pltpu.make_async_remote_copy(
            src_ref=block(shard),
            dst_ref=block(shard),
            send_sem=send_sem.at[0],
            recv_sem=recv_sem.at[shard],
            device_id=sibling,
            device_id_type=MESH,
        ).wait_recv()

    own = number(z, x, y, core)
    for partner in partners:
        send(mine_ref, own, partner)
    local = pltpu.make_async_copy(mine_ref, block(own), local_sem)
    local.start()

    def far(height):
        for at_x, at_y in ((second_x, second_y), (1 - x, 1 - y)):
            shard = number(height, at_x, at_y, core)
            arrive(shard)
            send(block(shard), shard, sibling)

    for step, height in enumerate(heights):
        if step:
            shard = number(height, x, y, core)
            arrive(shard)
            for partner in (first, second, sibling):
                send(block(shard), shard, partner)
        shard = number(height, first_x, first_y, core)
        arrive(shard)
        for partner in (second, sibling):
            send(block(shard), shard, partner)
        if step:
            far(heights[step - 1])
    far(heights[-1])
    for height in heights:
        for at_x, at_y in ((x, y), (first_x, first_y), (second_x, second_y), (1 - x, 1 - y)):
            arrive(number(height, at_x, at_y, 1 - core))
    local.wait()
    for copy in started:
        copy.wait_send()


def gathered(block):
    devices = lax.axis_size(("sta", "tpl"))
    if (lax.axis_size("sta"), lax.axis_size("tpl")) != (8, 4):
        return lax.all_gather(block, ("sta", "tpl"), axis=0, tiled=True)
    return pl.pallas_call(
        gather_kernel,
        in_specs=[pl.BlockSpec(memory_space=pl.ANY)],
        out_specs=pl.BlockSpec(memory_space=pl.ANY),
        out_shape=jax.ShapeDtypeStruct((devices * block.shape[0],) + block.shape[1:], block.dtype),
        scratch_shapes=[
            pltpu.SemaphoreType.DMA,
            pltpu.SemaphoreType.DMA((devices - 1,)),
            pltpu.SemaphoreType.DMA((devices,)),
        ],
        compiler_params=pltpu.CompilerParams(collective_id=0, has_side_effects=True),
    )(block)


def on_device(records, templates, pick_owner, pick_local, moveout, channel_mask):
    own_stations, channels, record_len = records.shape
    own_templates, picks, _, shape_len = templates.shape
    pieces = record_len // LANES
    frame_len = 3 * LANES
    blocks = (record_len - frame_len) // LANES
    held = -(-channels * pieces // 16) * 16
    everywhere = gathered(
        jnp.pad(
            records.reshape(own_stations, channels * pieces, LANES),
            ((0, 0), (0, held - channels * pieces), (0, 0)),
        )
    )
    station = (pick_owner * own_stations + pick_local).reshape(-1)
    power = jnp.sum(jnp.square(templates.astype(jnp.float32)), axis=3).reshape(-1)
    mask = channel_mask.astype(jnp.float32).reshape(-1)
    items = picks * channels
    shapes = jnp.pad(
        templates.reshape(own_templates, items, shape_len),
        ((0, 0), (0, -items % 16), (0, 2 * LANES - shape_len)),
    )
    offsets = (
        jnp.arange(frame_len, dtype=jnp.int32)[:, None] - jnp.arange(LANES, dtype=jnp.int32)[None, :]
    )
    band = ((offsets >= 0) & (offsets < shape_len)).astype(jnp.bfloat16)

    def record_spec(pick):
        return pl.BlockSpec(
            (1, held, LANES),
            lambda t, station, shift, power, mask: (station[t * picks + pick], 0, 0),
        )

    stacked = pl.pallas_call(
        functools.partial(stack_kernel, picks, channels, pieces),
        grid_spec=pltpu.PrefetchScalarGridSpec(
            num_scalar_prefetch=4,
            grid=(own_templates,),
            in_specs=[
                pl.BlockSpec((frame_len, LANES), lambda t, *_: (0, 0)),
                pl.BlockSpec((1,) + shapes.shape[1:], lambda t, *_: (t, 0, 0)),
            ]
            + [record_spec(pick) for pick in range(picks)],
            out_specs=pl.BlockSpec((1, blocks, LANES), lambda t, *_: (t, 0, 0)),
            scratch_shapes=[
                pltpu.VMEM((picks, held + 8, LANES), jnp.float32),
                pltpu.VMEM((items * blocks, frame_len), jnp.bfloat16),
                pltpu.VMEM((items * blocks, LANES), jnp.float32),
            ],
        ),
        out_shape=jax.ShapeDtypeStruct((own_templates, blocks, LANES), jnp.float32),
        compiler_params=pltpu.CompilerParams(vmem_limit_bytes=48 * 1024 * 1024),
    )(station, moveout.reshape(-1), power, mask, band, shapes, *([everywhere] * picks))
    return stacked.reshape(own_templates, blocks * LANES)


def solution(mesh):
    return jax.shard_map(
        on_device,
        mesh=mesh,
        in_specs=(
            P(("sta", "tpl"), None, None),
            P(("sta", "tpl"), None, None, None),
            P(("sta", "tpl"), None),
            P(("sta", "tpl"), None),
            P(("sta", "tpl"), None),
            P(("sta", "tpl"), None, None),
        ),
        out_specs=P(("sta", "tpl"), None),
        check_vma=False,
    )
```

time: 180 us -> 107 us (0.59)
  waiting for transfers between devices: 83.6 us -> 0 us
  Pallas kernels: 65.9 us -> 98.4 us
  between operations: 13.5 us -> 0.08 us
  local copies, waits for them, and re-layouts: 14.3 us -> 5.86 us
    all_gather x1 -> x0, waiting for transfers between devices: 82.9 us -> none  [on_device(): lax.all_gather(records.reshape(own_stations, channels * pieces, LANES), (...]
    pallas_call x1 -> x2, Pallas kernels: 65.9 us -> 98.4 us  [the longest x1 51.4 us: on_device(): pl.pallas_call(functools.partial(stack_kernel, picks, channels, pieces),...]
    all_gather x1 -> x0, local copies, waits for them, and re-layouts: 10.4 us -> none  [on_device(): lax.all_gather(records.reshape(own_stations, channels * pieces, LANES), (...]
  transfers between devices with their start and end apart: 1 -> 0, of which waited for: 1 -> 0; matrix products, arithmetic and copies ran while one was open for 3% -> 0% of each run, Pallas kernels for 0% -> 0%
where the time goes in v2:
time: 107 us
  Pallas kernels  98.4 us (92%)
  local copies, waits for them, and re-layouts  5.86 us (5%)
  other arithmetic  2.66 us (2%)
    pallas_call x1, Pallas kernels, on_device(): pl.pallas_call(functools.partial(stack_kernel, picks, channels, pieces),...  51.4 us
    pallas_call x1, Pallas kernels, gathered(): pl.pallas_call(gather_kernel, in_specs=[pl.BlockSpec(memory_space=pl.ANY)...  47 us
    unnamed x3, local copies, waits for them, and re-layouts  2.8 us

profile of v2, /device:TPU:0, one launch (start us, length us, event | category | flops | bytes accessed | tf_op | source)
XLA Modules:
  0.0 107.0 jit_solution(124538451014493419)
XLA Ops:
  0.0 0.7 multiply_add_fusion
  0.7 0.1 copy.20
  0.8 0.1 reshape.21.station
  0.9 0.8 copy.21
  1.7 0.1 reshape.22.shift
  1.8 1.2 %multiply_reduce_fusion = f32[24,10,3]{0,2,1:T(4,128)S(1)} fusion(bf16[24,10,3,200]{3,0,2,1:T(8,128)(2,1)} %param.7), kind=kLoop, calls=%fused_computation | loop fusion | flops 431280 | bytes 290880 | tf_op jit(solution)/shard_map/reduce_sum | solution.py:191
  3.0 0.7 copy_convert_fusion
  3.7 0.2 copy.24
  3.9 0.2 reshape.24.mask
  4.1 0.2 copy.22
  4.3 0.2 reshape.23.power
  4.5 1.0 copy.26
  5.5 0.2 reshape.26
  5.7 0.7 pad.9.mine_ref
  6.5 1.1 copy.25
  7.5 0.1 pad.8.shapes_ref
  7.6 47.0 %shard_map.64.rest_0_.rest_1_.rest_2_.rest_3_.rest_4_.rest_5_.rest_6_.rest_7_.rest_8_.rest_9_ = bf16[256,112,128]{2,1,0:T(8,128)(2,1)} custom-call(bf16[8,112,128]{2,1,0:T(8,128)(2,1)} %pad.9.mine_ref), custom_call_target="tpu_custom_call" | custom-call | tf_op jit(solution)/shard_map/pallas_call | solution.py:163
  54.7 51.4 %shard_map.65 = f32[24,32,128]{2,1,0:T(8,128)S(1)} custom-call(s32[240]{0:T(256)S(1)} %reshape.21.station, s32[240]{0:T(256)S(1)} %reshape.22.shift, f32[720]{0:T(1024)S(1)} %reshape.23.power, f32[720]{0:T(1024)S(1)} %reshape.24.mask, bf16[384,128]{1,0:T(8,128)(2,1)S(1)} %fusion.3.band_ref, bf16[24,32,256]{2,1,0:T(8,128)(2,1)S(1)} %pad.8.shapes_ref, ...), custom_call_target="tpu_custom_call" | custom-call | tf_op jit(solution)/shard_map/pallas_call | solution.py:209
  106.0 1.0 copy.30
  (1 shorter events, 0.0 us)

commit v3 on v2

--- a/solution.py
+++ b/solution.py
@@ -76,8 +76,13 @@
     out_ref[0] = total * lax.rsqrt(jnp.full((blocks, LANES), mean + EPS, jnp.float32))
 
 
-def gather_kernel(mine_ref, all_ref, local_sem, send_sem, recv_sem):
-    stations = mine_ref.shape[0]
+def fused_kernel(
+    picks, channels, pieces, base, shift, power, mask, band_ref, shapes_ref, mine_ref, out_ref, *scratch
+):
+    landed = scratch[:channels]
+    wide_ref, turned_ref, squares_ref, energy_ref, traces_ref, local_sem, send_sem, recv_sem = scratch[channels:]
+    templates, blocks = out_ref.shape[0], out_ref.shape[1]
+    devices, block_rows = landed[0].shape[0], landed[0].shape[1]
     sta, tpl = lax.axis_index("sta"), lax.axis_index("tpl")
     z, x, y, core = sta // 2, sta % 2, tpl // 2, tpl % 2
     first_x, first_y = x + (1 - core) * (1 - 2 * x), y + core * (1 - 2 * y)
@@ -88,90 +93,206 @@
     sibling = (sta, y * 2 + 1 - core)
     partners = [(height * 2 + x, tpl) for height in heights[1:]] + [first, second, sibling]
 
+    def number(height, at_x, at_y, at_core):
+        return (height * 2 + at_x) * 4 + at_y * 2 + at_core
+
+    own = number(z, x, y, core)
+    plan = [[(None, own, partner) for partner in partners]]
+    for step, height in enumerate(heights):
+        moves = []
+        shard = number(height, x, y, core)
+        if step:
+            moves += [(shard, None, None)]
+            moves += [(None, shard, partner) for partner in (first, second, sibling)]
+        shard = number(height, first_x, first_y, core)
+        moves += [(shard, None, None)]
+        moves += [(None, shard, partner) for partner in (second, sibling)]
+        plan.append(moves)
+    for step, height in enumerate(heights):
+        moves = plan[min(step + 2, 4)] if step < 3 else []
+        for at_x, at_y in ((second_x, second_y), (1 - x, 1 - y)):
+            shard = number(height, at_x, at_y, core)
+            moves += [(shard, None, None), (None, shard, sibling)]
+        if step == 3:
+            plan.append(moves)
+    last = []
+    for height in heights:
+        for at_x, at_y in ((x, y), (first_x, first_y), (second_x, second_y), (1 - x, 1 - y)):
+            last.append((number(height, at_x, at_y, 1 - core), None, None))
+    plan.append(last)
+    firsts = [sum(move[0] is None for moves in plan[:k] for move in moves) for k in range(len(plan))]
+
+    def copy_of(channel, index, shard, partner, source=None):
+        place = landed[channel].at[shard]
+        return pltpu.make_async_remote_copy(
+            src_ref=place if source is None else source,
+            dst_ref=place,
+            send_sem=send_sem.at[channel, index],
+            recv_sem=recv_sem.at[channel, shard],
+            device_id=partner,
+            device_id_type=MESH,
+        )
+
+    def run(channel, part):
+        index = firsts[part]
+        for arrival, shard, partner in plan[part]:
+            if arrival is not None:
+                copy_of(channel, 0, arrival, sibling).wait_recv()
+            else:
+                copy_of(
+                    channel, index, shard, partner, mine_ref.at[channel] if part == 0 else None
+                ).start()
+                index += 1
+
+    def local(channel):
+        return pltpu.make_async_copy(
+            mine_ref.at[channel], landed[channel].at[own], local_sem.at[channel]
+        )
+
     barrier = pltpu.get_barrier_semaphore()
     for partner in partners:
         pl.semaphore_signal(barrier, inc=1, device_id=partner, device_id_type=MESH)
     pl.semaphore_wait(barrier, len(partners))
-
-    def number(height, at_x, at_y, at_core):
-        return (height * 2 + at_x) * 4 + at_y * 2 + at_core
-
-    def block(shard):
-        return all_ref.at[pl.ds(shard * stations, stations)]
-
-    started = []
-
-    def send(source, shard, partner):
-        copy = pltpu.make_async_remote_copy(
-            src_ref=source,
-            dst_ref=block(shard),
-            send_sem=send_sem.at[len(started)],
-            recv_sem=recv_sem.at[shard],
-            device_id=partner,
-            device_id_type=MESH,
-        )
-        copy.start()
-        started.append(copy)
-
-    def arrive(shard):
-        pltpu.make_async_remote_copy(
-            src_ref=block(shard),
-            dst_ref=block(shard),
-            send_sem=send_sem.at[0],
-            recv_sem=recv_sem.at[shard],
-            device_id=sibling,
-            device_id_type=MESH,
-        ).wait_recv()
-
-    own = number(z, x, y, core)
-    for partner in partners:
-        send(mine_ref, own, partner)
-    local = pltpu.make_async_copy(mine_ref, block(own), local_sem)
-    local.start()
-
-    def far(height):
-        for at_x, at_y in ((second_x, second_y), (1 - x, 1 - y)):
-            shard = number(height, at_x, at_y, core)
-            arrive(shard)
-            send(block(shard), shard, sibling)
-
-    for step, height in enumerate(heights):
-        if step:
-            shard = number(height, x, y, core)
-            arrive(shard)
-            for partner in (first, second, sibling):
-                send(block(shard), shard, partner)
-        shard = number(height, first_x, first_y, core)
-        arrive(shard)
-        for partner in (second, sibling):
-            send(block(shard), shard, partner)
-        if step:
-            far(heights[step - 1])
-    far(heights[-1])
-    for height in heights:
-        for at_x, at_y in ((x, y), (first_x, first_y), (second_x, second_y), (1 - x, 1 - y)):
-            arrive(number(height, at_x, at_y, 1 - core))
-    local.wait()
-    for copy in started:
-        copy.wait_send()
-
-
-def gathered(block):
+    for channel in range(channels):
+        local(channel).start()
+    run(0, 0)
+    for part in (1, 2):
+        run(0, part)
+    run(1, 0)
+    for part in (3, 4, 5):
+        run(0, part)
+
+    lane = lax.broadcasted_iota(jnp.int32, (blocks, LANES), 1)
+    for channel in range(channels):
+        run(channel, 6)
+        local(channel).wait()
+
+        def widen(device, carry, channel=channel):
+            at = pl.multiple_of(device * block_rows, 16)
+            wide_ref[pl.ds(at, block_rows)] = landed[channel][device].astype(jnp.float32)
+            return carry
+
+        lax.fori_loop(0, devices, widen, 0)
+
+        def stack(template, carry, channel=channel):
+            if channel + 1 < channels:
+                for part in range(1, 6):
+
+                    @pl.when(template == 4 * part - 3)
+                    def _(part=part):
+                        run(channel + 1, part)
+
+            if channel + 2 < channels:
+
+                @pl.when(template == 10)
+                def _():
+                    run(channel + 2, 0)
+
+            shapes = shapes_ref[channel, template].astype(jnp.float32)
+            windows = []
+            for pick in range(picks):
+                item = template * picks + pick
+                moved = shift[item]
+                turned_ref[pick] = pltpu.roll(
+                    wide_ref[pl.ds(base[item], turned_ref.shape[1])],
+                    lax.rem(LANES - moved, LANES),
+                    axis=1,
+                )
+                window = jnp.concatenate(
+                    [
+                        jnp.where(
+                            lane < LANES - moved,
+                            turned_ref[pick, k : k + blocks],
+                            turned_ref[pick, k + 1 : k + 1 + blocks],
+                        ).astype(jnp.bfloat16)
+                        for k in range(3)
+                    ],
+                    axis=1,
+                )
+                windows.append(window)
+                squares_ref[pick * blocks : (pick + 1) * blocks] = window * window
+            energy_ref[...] = jnp.dot(
+                squares_ref[...], band_ref[...], preferred_element_type=jnp.float32
+            )
+            total = jnp.zeros((blocks, LANES), jnp.float32)
+            for pick in range(picks):
+                item = template * picks + pick
+                correlation = lax.dot_general(
+                    windows[pick],
+                    toeplitz(shapes[pick : pick + 1]),
+                    (((1,), (1,)), ((), ())),
+                    preferred_element_type=jnp.float32,
+                )
+                at = item * channels + channel
+                scale = lax.rsqrt(
+                    power[at] * energy_ref[pick * blocks : (pick + 1) * blocks] + EPS
+                )
+                trace = mask[at] * (correlation * scale)
+                if channel:
+                    trace = trace + traces_ref[item]
+                if channel + 1 < channels:
+                    traces_ref[item] = trace
+                else:
+                    total = total + trace.astype(jnp.bfloat16).astype(jnp.float32)
+            if channel + 1 == channels:
+                mean = jnp.sum(total * total) / (blocks * LANES)
+                out_ref[template] = total * lax.rsqrt(
+                    jnp.full((blocks, LANES), mean + EPS, jnp.float32)
+                )
+            return carry
+
+        lax.fori_loop(0, templates, stack, 0)
+    for channel in range(channels):
+        index = 0
+        for part, moves in enumerate(plan):
+            for arrival, shard, partner in moves:
+                if arrival is None:
+                    copy_of(
+                        channel, index, shard, partner, mine_ref.at[channel] if part == 0 else None
+                    ).wait_send()
+                    index += 1
+
+
+def fused(records, templates, pick_owner, pick_local, moveout, power, mask, band):
     devices = lax.axis_size(("sta", "tpl"))
-    if (lax.axis_size("sta"), lax.axis_size("tpl")) != (8, 4):
-        return lax.all_gather(block, ("sta", "tpl"), axis=0, tiled=True)
+    own_stations, channels, record_len = records.shape
+    own_templates, picks, _, shape_len = templates.shape
+    pieces = record_len // LANES
+    blocks = record_len // LANES - 3
+    block_rows = -(-own_stations * pieces // 16) * 16
+    mine = jnp.pad(
+        jnp.transpose(records.reshape(own_stations, channels, pieces, LANES), (1, 0, 2, 3)).reshape(
+            channels, own_stations * pieces, LANES
+        ),
+        ((0, 0), (0, block_rows - own_stations * pieces), (0, 0)),
+    )
+    shapes = jnp.pad(
+        jnp.transpose(templates, (2, 0, 1, 3)),
+        ((0, 0), (0, 0), (0, -picks % 16), (0, 2 * LANES - shape_len)),
+    )
+    base = (pick_owner * block_rows + pick_local * pieces).reshape(-1)
+    smem = pl.BlockSpec(memory_space=pltpu.SMEM)
+    vmem = pl.BlockSpec(memory_space=pltpu.VMEM)
     return pl.pallas_call(
-        gather_kernel,
-        in_specs=[pl.BlockSpec(memory_space=pl.ANY)],
-        out_specs=pl.BlockSpec(memory_space=pl.ANY),
-        out_shape=jax.ShapeDtypeStruct((devices * block.shape[0],) + block.shape[1:], block.dtype),
-        scratch_shapes=[
-            pltpu.SemaphoreType.DMA,
-            pltpu.SemaphoreType.DMA((devices - 1,)),
-            pltpu.SemaphoreType.DMA((devices,)),
+        functools.partial(fused_kernel, picks, channels, pieces),
+        in_specs=[smem] * 4 + [vmem] * 2 + [pl.BlockSpec(memory_space=pl.ANY)],
+        out_specs=vmem,
+        out_shape=jax.ShapeDtypeStruct((own_templates, blocks, LANES), jnp.float32),
+        scratch_shapes=[pltpu.VMEM((devices, block_rows, LANES), jnp.bfloat16)] * channels
+        + [
+            pltpu.VMEM((devices * block_rows, LANES), jnp.float32),
+            pltpu.VMEM((picks, blocks + 8, LANES), jnp.float32),
+            pltpu.VMEM((picks * blocks, 3 * LANES), jnp.bfloat16),
+            pltpu.VMEM((picks * blocks, LANES), jnp.float32),
+            pltpu.VMEM((own_templates * picks, blocks, LANES), jnp.float32),
+            pltpu.SemaphoreType.DMA((channels,)),
+            pltpu.SemaphoreType.DMA((channels, devices - 1)),
+            pltpu.SemaphoreType.DMA((channels, devices)),
         ],
-        compiler_params=pltpu.CompilerParams(collective_id=0, has_side_effects=True),
-    )(block)
+        compiler_params=pltpu.CompilerParams(
+            collective_id=0, has_side_effects=True, vmem_limit_bytes=48 * 1024 * 1024
+        ),
+    )(base, moveout.reshape(-1), power, mask, band, shapes, mine)
 
 
 def on_device(records, templates, pick_owner, pick_local, moveout, channel_mask):
@@ -180,25 +301,33 @@
     pieces = record_len // LANES
     frame_len = 3 * LANES
     blocks = (record_len - frame_len) // LANES
+    power = jnp.sum(jnp.square(templates.astype(jnp.float32)), axis=3).reshape(-1)
+    mask = channel_mask.astype(jnp.float32).reshape(-1)
+    offsets = (
+        jnp.arange(frame_len, dtype=jnp.int32)[:, None] - jnp.arange(LANES, dtype=jnp.int32)[None, :]
+    )
+    band = ((offsets >= 0) & (offsets < shape_len)).astype(jnp.bfloat16)
+
+    if (lax.axis_size("sta"), lax.axis_size("tpl"), channels) == (8, 4, 3):
+        stacked = fused(records, templates, pick_owner, pick_local, moveout, power, mask, band)
+        return stacked.reshape(own_templates, blocks * LANES)
+
     held = -(-channels * pieces // 16) * 16
-    everywhere = gathered(
+    everywhere = lax.all_gather(
         jnp.pad(
             records.reshape(own_stations, channels * pieces, LANES),
             ((0, 0), (0, held - channels * pieces), (0, 0)),
-        )
+        ),
+        ("sta", "tpl"),
+        axis=0,
+        tiled=True,
     )
     station = (pick_owner * own_stations + pick_local).reshape(-1)
-    power = jnp.sum(jnp.square(templates.astype(jnp.float32)), axis=3).reshape(-1)
-    mask = channel_mask.astype(jnp.float32).reshape(-1)
     items = picks * channels
     shapes = jnp.pad(
         templates.reshape(own_templates, items, shape_len),
         ((0, 0), (0, -items % 16), (0, 2 * LANES - shape_len)),
     )
-    offsets = (
-        jnp.arange(frame_len, dtype=jnp.int32)[:, None] - jnp.arange(LANES, dtype=jnp.int32)[None, :]
-    )
-    band = ((offsets >= 0) & (offsets < shape_len)).astype(jnp.bfloat16)
 
     def record_spec(pick):
         return pl.BlockSpec(

time: 107 us -> 126 us (1.18)
  Pallas kernels: 98.4 us -> 119 us
  other arithmetic: 2.66 us -> 0.23 us
    pallas_call x2 -> x1, Pallas kernels: 98.4 us -> 119 us  [fused(): pl.pallas_call(functools.partial(fused_kernel, picks, channels, pieces),...]
    unnamed x3 -> x15, local copies, waits for them, and re-layouts: 2.8 us -> 4.9 us
where the time goes in v3:
time: 126 us; the launch traced here: 125 us
  Pallas kernels  119 us (94%)
  local copies, waits for them, and re-layouts  6.19 us (5%)
    pallas_call x1, Pallas kernels, fused(): pl.pallas_call(functools.partial(fused_kernel, picks, channels, pieces),...  119 us
    unnamed x15, local copies, waits for them, and re-layouts  4.9 us

profile of v3, /device:TPU:0, one launch (start us, length us, event | category | flops | bytes accessed | tf_op | source)
XLA Modules:
  0.0 125.5 jit_solution(8059346325945356121)
XLA Ops:
  0.0 1.1 copy.32
  1.1 0.0 copy-start.1
  1.1 0.1 pad.8.shapes_ref
  1.2 0.8 copy-done.1
  2.1 0.1 reshape.26
  2.2 0.0 copy-start.2
  2.2 0.0 copy-start
  2.2 0.7 copy-done.2
  2.9 0.2 copy.24
  3.1 0.2 reshape.24.mask
  3.3 0.2 multiply_reduce_fusion
  3.5 0.2 copy.22
  3.7 0.2 reshape.23.power
  3.9 0.0 copy-start.3
  3.9 0.0 copy-start.4
  3.9 0.6 copy-done.3
  4.6 0.0 copy-done.4
  4.6 0.1 copy.20
  4.7 0.1 reshape.21.base
  4.8 0.6 copy-done.5
  5.4 0.1 copy.21
  5.5 0.1 reshape.22.shift
  5.6 118.9 %shard_map.64 = f32[24,32,128]{2,1,0:T(8,128)S(1)} custom-call(s32[240]{0:T(256)S(1)} %reshape.21.base, s32[240]{0:T(256)S(1)} %reshape.22.shift, f32[720]{0:T(1024)S(1)} %reshape.23.power, f32[720]{0:T(1024)S(1)} %reshape.24.mask, bf16[384,128]{1,0:T(8,128)(2,1)S(1)} %fusion.3.band_ref, bf16[3,24,16,256]{3,2,1,0:T(8,128)(2,1)S(1)} %pad.8.shapes_ref, ...), custom_call_target="tpu_custom_call" | custom-call | tf_op jit(solution)/shard_map/pallas_call | solution.py:276
  124.5 1.0 copy.33
  (7 shorter events, 0.1 us)
Async XLA Ops:
  1.1 0.9 copy-start.1
  2.2 0.7 copy-start.2
  2.2 1.1 copy-start
  3.9 0.7 copy-start.3
  3.9 0.7 copy-start.4
  4.7 0.7 copy-start.5

commit v4 on v3

--- a/solution.py
+++ b/solution.py
@@ -9,6 +9,7 @@
 
 EPS = 1e-06
 LANES = 128
+GROUP = 6
 MESH = pl.DeviceIdType.MESH
 
 
@@ -80,7 +81,7 @@
     picks, channels, pieces, base, shift, power, mask, band_ref, shapes_ref, mine_ref, out_ref, *scratch
 ):
     landed = scratch[:channels]
-    wide_ref, turned_ref, squares_ref, energy_ref, traces_ref, local_sem, send_sem, recv_sem = scratch[channels:]
+    wide_ref, turned_ref, windows_ref, energy_ref, traces_ref, local_sem, send_sem, recv_sem = scratch[channels:]
     templates, blocks = out_ref.shape[0], out_ref.shape[1]
     devices, block_rows = landed[0].shape[0], landed[0].shape[1]
     sta, tpl = lax.axis_index("sta"), lax.axis_index("tpl")
@@ -174,58 +175,45 @@
 
         lax.fori_loop(0, devices, widen, 0)
 
-        def stack(template, carry, channel=channel):
-            if channel + 1 < channels:
-                for part in range(1, 6):
-
-                    @pl.when(template == 4 * part - 3)
-                    def _(part=part):
-                        run(channel + 1, part)
-
-            if channel + 2 < channels:
-
-                @pl.when(template == 10)
-                def _():
-                    run(channel + 2, 0)
-
-            shapes = shapes_ref[channel, template].astype(jnp.float32)
-            windows = []
+        def prepare(template, slot):
             for pick in range(picks):
                 item = template * picks + pick
                 moved = shift[item]
-                turned_ref[pick] = pltpu.roll(
-                    wide_ref[pl.ds(base[item], turned_ref.shape[1])],
+                turned_ref[slot, pick] = pltpu.roll(
+                    wide_ref[pl.ds(base[item], turned_ref.shape[2])],
                     lax.rem(LANES - moved, LANES),
                     axis=1,
                 )
-                window = jnp.concatenate(
+                windows_ref[slot, pick * blocks : (pick + 1) * blocks] = jnp.concatenate(
                     [
                         jnp.where(
                             lane < LANES - moved,
-                            turned_ref[pick, k : k + blocks],
-                            turned_ref[pick, k + 1 : k + 1 + blocks],
+                            turned_ref[slot, pick, k : k + blocks],
+                            turned_ref[slot, pick, k + 1 : k + 1 + blocks],
                         ).astype(jnp.bfloat16)
                         for k in range(3)
                     ],
                     axis=1,
                 )
-                windows.append(window)
-                squares_ref[pick * blocks : (pick + 1) * blocks] = window * window
-            energy_ref[...] = jnp.dot(
-                squares_ref[...], band_ref[...], preferred_element_type=jnp.float32
+            windows = windows_ref[slot]
+            energy_ref[slot] = jnp.dot(
+                windows * windows, band_ref[...], preferred_element_type=jnp.float32
             )
+
+        def combine(template, slot, channel):
+            shapes = shapes_ref[channel, template].astype(jnp.float32)
             total = jnp.zeros((blocks, LANES), jnp.float32)
             for pick in range(picks):
                 item = template * picks + pick
                 correlation = lax.dot_general(
-                    windows[pick],
+                    windows_ref[slot, pick * blocks : (pick + 1) * blocks],
                     toeplitz(shapes[pick : pick + 1]),
                     (((1,), (1,)), ((), ())),
                     preferred_element_type=jnp.float32,
                 )
                 at = item * channels + channel
                 scale = lax.rsqrt(
-                    power[at] * energy_ref[pick * blocks : (pick + 1) * blocks] + EPS
+                    power[at] * energy_ref[slot, pick * blocks : (pick + 1) * blocks] + EPS
                 )
                 trace = mask[at] * (correlation * scale)
                 if channel:
@@ -239,9 +227,26 @@
                 out_ref[template] = total * lax.rsqrt(
                     jnp.full((blocks, LANES), mean + EPS, jnp.float32)
                 )
+
+        def stack(step, carry, channel=channel):
+            if channel + 1 < channels:
+                for at, parts in enumerate(((1,), (2, 3), (4,), (5,))):
+
+                    @pl.when(step == at)
+                    def _(parts=parts, at=at):
+                        for part in parts:
+                            run(channel + 1, part)
+                        if channel + 2 < channels and at == 2:
+                            run(channel + 2, 0)
+
+            prepare(step * GROUP, 0)
+            for slot in range(GROUP):
+                if slot + 1 < GROUP:
+                    prepare(step * GROUP + slot + 1, slot + 1)
+                combine(step * GROUP + slot, slot, channel)
             return carry
 
-        lax.fori_loop(0, templates, stack, 0)
+        lax.fori_loop(0, templates // GROUP, stack, 0)
     for channel in range(channels):
         index = 0
         for part, moves in enumerate(plan):
@@ -281,9 +286,9 @@
         scratch_shapes=[pltpu.VMEM((devices, block_rows, LANES), jnp.bfloat16)] * channels
         + [
             pltpu.VMEM((devices * block_rows, LANES), jnp.float32),
-            pltpu.VMEM((picks, blocks + 8, LANES), jnp.float32),
-            pltpu.VMEM((picks * blocks, 3 * LANES), jnp.bfloat16),
-            pltpu.VMEM((picks * blocks, LANES), jnp.float32),
+            pltpu.VMEM((GROUP, picks, blocks + 8, LANES), jnp.float32),
+            pltpu.VMEM((GROUP, picks * blocks, 3 * LANES), jnp.bfloat16),
+            pltpu.VMEM((GROUP, picks * blocks, LANES), jnp.float32),
             pltpu.VMEM((own_templates * picks, blocks, LANES), jnp.float32),
             pltpu.SemaphoreType.DMA((channels,)),
             pltpu.SemaphoreType.DMA((channels, devices - 1)),
@@ -308,7 +313,8 @@
     )
     band = ((offsets >= 0) & (offsets < shape_len)).astype(jnp.bfloat16)
 
-    if (lax.axis_size("sta"), lax.axis_size("tpl"), channels) == (8, 4, 3):
+    small = (lax.axis_size("sta"), lax.axis_size("tpl"), channels) == (8, 4, 3)
+    if small and own_templates == 4 * GROUP:
         stacked = fused(records, templates, pick_owner, pick_local, moveout, power, mask, band)
         return stacked.reshape(own_templates, blocks * LANES)
 

time: 126 us -> 101 us (0.80)
  Pallas kernels: 119 us -> 94 us
    pallas_call x1, Pallas kernels: 119 us -> 94 us  [fused(): pl.pallas_call(functools.partial(fused_kernel, picks, channels, pieces),...]
where the time goes in v4:
time: 101 us
  Pallas kernels  94 us (93%)
  local copies, waits for them, and re-layouts  6.19 us (6%)
    pallas_call x1, Pallas kernels, fused(): pl.pallas_call(functools.partial(fused_kernel, picks, channels, pieces),...  94 us
    unnamed x15, local copies, waits for them, and re-layouts  4.9 us

profile of v4, /device:TPU:0, one launch (start us, length us, event | category | flops | bytes accessed | tf_op | source)
XLA Modules:
  0.0 100.5 jit_solution(13117208833485790294)
XLA Ops:
  0.0 1.1 %copy.32 = bf16[24,10,3,200]{3,1,0,2:T(8,128)(2,1)S(1)} copy(bf16[24,10,3,200]{3,0,2,1:T(8,128)(2,1)} %param.7) | data formatting | bytes 576000 | tf_op args[1]
  1.1 0.0 copy-start.1
  1.1 0.1 pad.8.shapes_ref
  1.2 0.8 copy-done.1
  2.1 0.1 reshape.26
  2.2 0.0 copy-start.2
  2.2 0.0 copy-start
  2.2 0.7 copy-done.2
  2.9 0.2 copy.24
  3.1 0.2 reshape.24.mask
  3.3 0.2 multiply_reduce_fusion
  3.5 0.2 copy.22
  3.7 0.2 reshape.23.power
  3.9 0.0 copy-start.3
  3.9 0.0 copy-start.4
  3.9 0.6 copy-done.3
  4.6 0.0 copy-done.4
  4.6 0.1 copy.20
  4.7 0.1 reshape.21.base
  4.8 0.6 copy-done.5
  5.4 0.1 copy.21
  5.5 0.1 reshape.22.shift
  5.6 94.0 %shard_map.64 = f32[24,32,128]{2,1,0:T(8,128)S(1)} custom-call(s32[240]{0:T(256)S(1)} %reshape.21.base, s32[240]{0:T(256)S(1)} %reshape.22.shift, f32[720]{0:T(1024)S(1)} %reshape.23.power, f32[720]{0:T(1024)S(1)} %reshape.24.mask, bf16[384,128]{1,0:T(8,128)(2,1)S(1)} %fusion.3.band_ref, bf16[3,24,16,256]{3,2,1,0:T(8,128)(2,1)S(1)} %pad.8.shapes_ref, ...), custom_call_target="tpu_custom_call" | custom-call | tf_op jit(solution)/shard_map/pallas_call | solution.py:281
  99.5 1.0 copy.33
  (7 shorter events, 0.1 us)
Async XLA Ops:
  1.1 0.9 copy-start.1
  2.2 0.7 copy-start.2
  2.2 1.1 %copy-start = (bf16[24,10,3,200]{3,0,2,1:T(8,128)(2,1)S(1)}, bf16[24,10,3,200]{3,0,2,1:T(8,128)(2,1)}, u32[]{:S(2)}) copy-start(bf16[24,10,3,200]{3,0,2,1:T(8,128)(2,1)} %param.7) | copy-start | bytes 864004
  3.9 0.7 copy-start.3
  3.9 0.7 copy-start.4
  4.7 0.7 copy-start.5

commit v5 on v4

--- a/solution.py
+++ b/solution.py
@@ -81,7 +81,7 @@
     picks, channels, pieces, base, shift, power, mask, band_ref, shapes_ref, mine_ref, out_ref, *scratch
 ):
     landed = scratch[:channels]
-    wide_ref, turned_ref, windows_ref, energy_ref, traces_ref, local_sem, send_sem, recv_sem = scratch[channels:]
+    wide_ref, turned_ref, windows_ref, energy_ref, traces_ref, tables_ref, local_sem, send_sem, recv_sem = scratch[channels:]
     templates, blocks = out_ref.shape[0], out_ref.shape[1]
     devices, block_rows = landed[0].shape[0], landed[0].shape[1]
     sta, tpl = lax.axis_index("sta"), lax.axis_index("tpl")
@@ -98,29 +98,33 @@
         return (height * 2 + at_x) * 4 + at_y * 2 + at_core
 
     own = number(z, x, y, core)
-    plan = [[(None, own, partner) for partner in partners]]
-    for step, height in enumerate(heights):
-        moves = []
-        shard = number(height, x, y, core)
-        if step:
-            moves += [(shard, None, None)]
-            moves += [(None, shard, partner) for partner in (first, second, sibling)]
-        shard = number(height, first_x, first_y, core)
-        moves += [(shard, None, None)]
-        moves += [(None, shard, partner) for partner in (second, sibling)]
-        plan.append(moves)
-    for step, height in enumerate(heights):
-        moves = plan[min(step + 2, 4)] if step < 3 else []
-        for at_x, at_y in ((second_x, second_y), (1 - x, 1 - y)):
-            shard = number(height, at_x, at_y, core)
-            moves += [(shard, None, None), (None, shard, sibling)]
-        if step == 3:
-            plan.append(moves)
-    last = []
-    for height in heights:
-        for at_x, at_y in ((x, y), (first_x, first_y), (second_x, second_y), (1 - x, 1 - y)):
-            last.append((number(height, at_x, at_y, 1 - core), None, None))
-    plan.append(last)
+    def wait(height, at_x, at_y, onward):
+        shard = number(height, at_x, at_y, core)
+        return [(shard, None, None)] + [(None, shard, partner) for partner in onward]
+
+    def straight(step):
+        return wait(heights[step], x, y, (first, second, sibling))
+
+    def by_first(step):
+        return wait(heights[step], first_x, first_y, (second, sibling))
+
+    def by_second(step):
+        return wait(heights[step], second_x, second_y, (sibling,))
+
+    def by_both(step):
+        return wait(heights[step], 1 - x, 1 - y, (sibling,))
+
+    plan = [
+        [(None, own, partner) for partner in partners],
+        by_first(0) + by_second(0) + straight(1) + straight(2) + straight(3),
+        by_first(1) + by_both(0) + by_second(1) + by_first(2) + by_second(2) + by_first(3) + by_second(3),
+        by_both(1) + by_both(2) + by_both(3),
+        [
+            (number(height, at_x, at_y, 1 - core), None, None)
+            for height in heights
+            for at_x, at_y in ((x, y), (first_x, first_y), (second_x, second_y), (1 - x, 1 - y))
+        ],
+    ]
     firsts = [sum(move[0] is None for moves in plan[:k] for move in moves) for k in range(len(plan))]
 
     def copy_of(channel, index, shard, partner, source=None):
@@ -157,15 +161,27 @@
     for channel in range(channels):
         local(channel).start()
     run(0, 0)
-    for part in (1, 2):
-        run(0, part)
+    third = templates // 3
+
+    def tabulate(template, carry):
+        for part in (1, 2):
+
+            @pl.when(template == part * third)
+            def _(part=part):
+                run(0, part)
+
+        shapes = shapes_ref[0, template].astype(jnp.float32)
+        for pick in range(picks):
+            tables_ref[template * picks + pick] = toeplitz(shapes[pick : pick + 1])
+        return carry
+
+    lax.fori_loop(0, templates, tabulate, 0)
     run(1, 0)
-    for part in (3, 4, 5):
-        run(0, part)
+    run(0, 3)
 
     lane = lax.broadcasted_iota(jnp.int32, (blocks, LANES), 1)
     for channel in range(channels):
-        run(channel, 6)
+        run(channel, 4)
         local(channel).wait()
 
         def widen(device, carry, channel=channel):
@@ -207,7 +223,7 @@
                 item = template * picks + pick
                 correlation = lax.dot_general(
                     windows_ref[slot, pick * blocks : (pick + 1) * blocks],
-                    toeplitz(shapes[pick : pick + 1]),
+                    toeplitz(shapes[pick : pick + 1]) if channel else tables_ref[item],
                     (((1,), (1,)), ((), ())),
                     preferred_element_type=jnp.float32,
                 )
@@ -230,13 +246,12 @@
 
         def stack(step, carry, channel=channel):
             if channel + 1 < channels:
-                for at, parts in enumerate(((1,), (2, 3), (4,), (5,))):
-
-                    @pl.when(step == at)
-                    def _(parts=parts, at=at):
-                        for part in parts:
-                            run(channel + 1, part)
-                        if channel + 2 < channels and at == 2:
+                for part in (1, 2, 3):
+
+                    @pl.when(step == part)
+                    def _(part=part):
+                        run(channel + 1, part)
+                        if channel + 2 < channels and part == 3:
                             run(channel + 2, 0)
 
             prepare(step * GROUP, 0)
@@ -290,12 +305,13 @@
             pltpu.VMEM((GROUP, picks * blocks, 3 * LANES), jnp.bfloat16),
             pltpu.VMEM((GROUP, picks * blocks, LANES), jnp.float32),
             pltpu.VMEM((own_templates * picks, blocks, LANES), jnp.float32),
+            pltpu.VMEM((own_templates * picks, LANES, 3 * LANES), jnp.bfloat16),
             pltpu.SemaphoreType.DMA((channels,)),
             pltpu.SemaphoreType.DMA((channels, devices - 1)),
             pltpu.SemaphoreType.DMA((channels, devices)),
         ],
         compiler_params=pltpu.CompilerParams(
-            collective_id=0, has_side_effects=True, vmem_limit_bytes=48 * 1024 * 1024
+            collective_id=0, has_side_effects=True, vmem_limit_bytes=56 * 1024 * 1024
         ),
     )(base, moveout.reshape(-1), power, mask, band, shapes, mine)
 

time: 101 us -> 86 us (0.85)
  Pallas kernels: 94 us -> 76.4 us
  local copies, waits for them, and re-layouts: 6.19 us -> 8.34 us
    pallas_call x1, Pallas kernels: 94 us -> 76.4 us  [fused(): pl.pallas_call(functools.partial(fused_kernel, picks, channels, pieces),...]
    unnamed x15, local copies, waits for them, and re-layouts: 4.9 us -> 3.22 us
where the time goes in v5:
time: 86 us; the launch traced here: 85.7 us
  Pallas kernels  76.4 us (89%)
  local copies, waits for them, and re-layouts  8.34 us (10%)
  other arithmetic  0.87 us (1%)
    pallas_call x1, Pallas kernels, fused(): pl.pallas_call(functools.partial(fused_kernel, picks, channels, pieces),...  76.4 us
    unnamed x15, local copies, waits for them, and re-layouts  3.22 us

profile of v5, /device:TPU:0, one launch (start us, length us, event | category | flops | bytes accessed | tf_op | source)
XLA Modules:
  0.0 85.7 jit_solution(15688774369396908951)
XLA Ops:
  0.0 1.1 %copy.32 = bf16[24,10,3,200]{3,1,0,2:T(8,128)(2,1)S(1)} copy(bf16[24,10,3,200]{3,0,2,1:T(8,128)(2,1)} %param.7) | data formatting | bytes 576000 | tf_op args[1]
  1.1 0.0 copy-start.1
  1.1 0.9 %pad.8.shapes_ref = bf16[3,24,16,256]{3,2,1,0:T(8,128)(2,1)} pad(bf16[3,24,10,200]{3,2,1,0:T(8,128)(2,1)S(1)} %bitcast.11, bf16[]{:T(256)} %constant.12.clone.1), padding=0_0x0_0x0_6x0_56 | pad | bytes 877826 | tf_op jit(solution)/shard_map/jit(_pad)/pad | solution.py:289
  2.0 0.0 copy-done.1
  2.1 0.1 reshape.26
  2.2 0.0 copy-start.2
  2.2 0.0 copy-start
  2.2 0.7 pad.9.mine_ref
  2.9 0.0 copy-done.2
  2.9 0.2 copy.24
  3.1 0.8 reshape.24.mask
  3.9 0.2 multiply_reduce_fusion
  4.1 0.2 copy.22
  4.3 0.8 reshape.23.power
  5.1 0.7 fusion.3.band_ref
  5.7 0.0 copy-done.3
  5.8 0.0 copy-done.4
  5.8 0.1 copy.20
  5.9 0.7 reshape.21.base
  6.5 0.0 copy-done.5
  6.6 0.1 copy.21
  6.6 0.7 reshape.22.shift
  7.3 76.4 %shard_map.64 = f32[24,32,128]{2,1,0:T(8,128)} custom-call(s32[240]{0:T(256)} %reshape.21.base, s32[240]{0:T(256)} %reshape.22.shift, f32[720]{0:T(1024)} %reshape.23.power, f32[720]{0:T(1024)} %reshape.24.mask, bf16[384,128]{1,0:T(8,128)(2,1)} %fusion.3.band_ref, bf16[3,24,16,256]{3,2,1,0:T(8,128)(2,1)} %pad.8.shapes_ref, bf16[3,288,128]{2,1,0:T(8,128)(2,1)} %pad.9.mine_ref), custom_call_target="tpu_custom_call" | custom-call | tf_op jit(solution)/shard_map/pallas_call | solution.py:296
  83.7 2.0 %copy.33 = f32[3,8,32,128]{3,1,2,0:T(8,128)} copy(f32[3,8,32,128]{3,2,1,0:T(8,128)} %bitcast.12) | data formatting | bytes 786432
  (7 shorter events, 0.1 us)
Async XLA Ops:
  1.1 0.9 %copy-start.1 = (bf16[8,3,4480]{2,0,1:T(8,128)(2,1)S(1)}, bf16[8,3,4480]{2,0,1:T(8,128)(2,1)}, u32[]{:S(2)}) copy-start(bf16[8,3,4480]{2,0,1:T(8,128)(2,1)} %param.6) | copy-start | bytes 645124
  2.2 0.7 copy-start.2
  2.2 1.7 %copy-start = (bf16[24,10,3,200]{3,0,2,1:T(8,128)(2,1)S(1)}, bf16[24,10,3,200]{3,0,2,1:T(8,128)(2,1)}, u32[]{:S(2)}) copy-start(bf16[24,10,3,200]{3,0,2,1:T(8,128)(2,1)} %param.7) | copy-start | bytes 864004
  5.1 0.7 copy-start.3
  5.1 0.7 copy-start.4
  5.9 0.7 copy-start.5

commit v6 on v5

--- a/solution.py
+++ b/solution.py
@@ -10,6 +10,7 @@
 EPS = 1e-06
 LANES = 128
 GROUP = 6
+EXTRA = 12
 MESH = pl.DeviceIdType.MESH
 
 
@@ -78,7 +79,7 @@
 
 
 def fused_kernel(
-    picks, channels, pieces, base, shift, power, mask, band_ref, shapes_ref, mine_ref, out_ref, *scratch
+    picks, channels, pieces, owner, place, shift, power, mask, band_ref, shapes_ref, mine_ref, out_ref, *scratch
 ):
     landed = scratch[:channels]
     wide_ref, turned_ref, windows_ref, energy_ref, traces_ref, tables_ref, local_sem, send_sem, recv_sem = scratch[channels:]
@@ -161,21 +162,23 @@
     for channel in range(channels):
         local(channel).start()
     run(0, 0)
-    third = templates // 3
-
-    def tabulate(template, carry):
+    ready = tables_ref.shape[0] // picks
+    third = ready // 3
+
+    def tabulate(entry, carry):
         for part in (1, 2):
 
-            @pl.when(template == part * third)
+            @pl.when(entry == part * third)
             def _(part=part):
                 run(0, part)
 
-        shapes = shapes_ref[0, template].astype(jnp.float32)
+        extra = entry // templates
+        shapes = shapes_ref[extra * (channels - 1), entry - extra * templates].astype(jnp.float32)
         for pick in range(picks):
-            tables_ref[template * picks + pick] = toeplitz(shapes[pick : pick + 1])
+            tables_ref[entry * picks + pick] = toeplitz(shapes[pick : pick + 1])
         return carry
 
-    lax.fori_loop(0, templates, tabulate, 0)
+    lax.fori_loop(0, ready, tabulate, 0)
     run(1, 0)
     run(0, 3)
 
@@ -193,10 +196,10 @@
 
         def prepare(template, slot):
             for pick in range(picks):
-                item = template * picks + pick
-                moved = shift[item]
+                moved = shift[template, pick]
+                base = owner[template, pick] * block_rows + place[template, pick] * pieces
                 turned_ref[slot, pick] = pltpu.roll(
-                    wide_ref[pl.ds(base[item], turned_ref.shape[2])],
+                    wide_ref[pl.ds(base, turned_ref.shape[2])],
                     lax.rem(LANES - moved, LANES),
                     axis=1,
                 )
@@ -216,22 +219,22 @@
                 windows * windows, band_ref[...], preferred_element_type=jnp.float32
             )
 
-        def combine(template, slot, channel):
+        def combine(template, slot, channel, start):
             shapes = shapes_ref[channel, template].astype(jnp.float32)
             total = jnp.zeros((blocks, LANES), jnp.float32)
             for pick in range(picks):
                 item = template * picks + pick
                 correlation = lax.dot_general(
                     windows_ref[slot, pick * blocks : (pick + 1) * blocks],
-                    toeplitz(shapes[pick : pick + 1]) if channel else tables_ref[item],
+                    toeplitz(shapes[pick : pick + 1]) if start is None else tables_ref[start + item],
                     (((1,), (1,)), ((), ())),
                     preferred_element_type=jnp.float32,
                 )
-                at = item * channels + channel
+                at = pick * channels + channel
                 scale = lax.rsqrt(
-                    power[at] * energy_ref[slot, pick * blocks : (pick + 1) * blocks] + EPS
+                    power[template, at] * energy_ref[slot, pick * blocks : (pick + 1) * blocks] + EPS
                 )
-                trace = mask[at] * (correlation * scale)
+                trace = mask[template, at] * (correlation * scale)
                 if channel:
                     trace = trace + traces_ref[item]
                 if channel + 1 < channels:
@@ -244,7 +247,7 @@
                     jnp.full((blocks, LANES), mean + EPS, jnp.float32)
                 )
 
-        def stack(step, carry, channel=channel):
+        def stack(step, carry, channel=channel, start=None):
             if channel + 1 < channels:
                 for part in (1, 2, 3):
 
@@ -258,10 +261,16 @@
             for slot in range(GROUP):
                 if slot + 1 < GROUP:
                     prepare(step * GROUP + slot + 1, slot + 1)
-                combine(step * GROUP + slot, slot, channel)
+                combine(step * GROUP + slot, slot, channel, start)
             return carry
 
-        lax.fori_loop(0, templates // GROUP, stack, 0)
+        steps = templates // GROUP
+        at_hand = (steps, 0, ready // GROUP - steps)[channel]
+        if at_hand:
+            start = templates * picks if channel else 0
+            lax.fori_loop(0, at_hand, functools.partial(stack, start=start), 0)
+        if at_hand < steps:
+            lax.fori_loop(at_hand, steps, stack, 0)
     for channel in range(channels):
         index = 0
         for part, moves in enumerate(plan):
@@ -290,12 +299,11 @@
         jnp.transpose(templates, (2, 0, 1, 3)),
         ((0, 0), (0, 0), (0, -picks % 16), (0, 2 * LANES - shape_len)),
     )
-    base = (pick_owner * block_rows + pick_local * pieces).reshape(-1)
     smem = pl.BlockSpec(memory_space=pltpu.SMEM)
     vmem = pl.BlockSpec(memory_space=pltpu.VMEM)
     return pl.pallas_call(
         functools.partial(fused_kernel, picks, channels, pieces),
-        in_specs=[smem] * 4 + [vmem] * 2 + [pl.BlockSpec(memory_space=pl.ANY)],
+        in_specs=[smem] * 5 + [vmem] * 2 + [pl.BlockSpec(memory_space=pl.ANY)],
         out_specs=vmem,
         out_shape=jax.ShapeDtypeStruct((own_templates, blocks, LANES), jnp.float32),
         scratch_shapes=[pltpu.VMEM((devices, block_rows, LANES), jnp.bfloat16)] * channels
@@ -305,15 +313,24 @@
             pltpu.VMEM((GROUP, picks * blocks, 3 * LANES), jnp.bfloat16),
             pltpu.VMEM((GROUP, picks * blocks, LANES), jnp.float32),
             pltpu.VMEM((own_templates * picks, blocks, LANES), jnp.float32),
-            pltpu.VMEM((own_templates * picks, LANES, 3 * LANES), jnp.bfloat16),
+            pltpu.VMEM(((own_templates + EXTRA) * picks, LANES, 3 * LANES), jnp.bfloat16),
             pltpu.SemaphoreType.DMA((channels,)),
             pltpu.SemaphoreType.DMA((channels, devices - 1)),
             pltpu.SemaphoreType.DMA((channels, devices)),
         ],
         compiler_params=pltpu.CompilerParams(
-            collective_id=0, has_side_effects=True, vmem_limit_bytes=56 * 1024 * 1024
+            collective_id=0, has_side_effects=True, vmem_limit_bytes=58 * 1024 * 1024
         ),
-    )(base, moveout.reshape(-1), power, mask, band, shapes, mine)
+    )(
+        pick_owner,
+        pick_local,
+        moveout,
+        power.reshape(own_templates, picks * channels),
+        mask.reshape(own_templates, picks * channels),
+        band,
+        shapes,
+        mine,
+    )
 
 
 def on_device(records, templates, pick_owner, pick_local, moveout, channel_mask):
@@ -322,8 +339,8 @@
     pieces = record_len // LANES
     frame_len = 3 * LANES
     blocks = (record_len - frame_len) // LANES
-    power = jnp.sum(jnp.square(templates.astype(jnp.float32)), axis=3).reshape(-1)
-    mask = channel_mask.astype(jnp.float32).reshape(-1)
+    power = jnp.sum(jnp.square(templates.astype(jnp.float32)), axis=3)
+    mask = channel_mask.astype(jnp.float32)
     offsets = (
         jnp.arange(frame_len, dtype=jnp.int32)[:, None] - jnp.arange(LANES, dtype=jnp.int32)[None, :]
     )
@@ -376,7 +393,7 @@
         ),
         out_shape=jax.ShapeDtypeStruct((own_templates, blocks, LANES), jnp.float32),
         compiler_params=pltpu.CompilerParams(vmem_limit_bytes=48 * 1024 * 1024),
-    )(station, moveout.reshape(-1), power, mask, band, shapes, *([everywhere] * picks))
+    )(station, moveout.reshape(-1), power.reshape(-1), mask.reshape(-1), band, shapes, *([everywhere] * picks))
     return stacked.reshape(own_templates, blocks * LANES)
 
 

time: 86 us -> 88.3 us (1.027)
  Pallas kernels: 76.4 us -> 78.6 us
    pallas_call x1, Pallas kernels: 76.4 us -> 78.6 us  [fused(): pl.pallas_call(functools.partial(fused_kernel, picks, channels, pieces),...]
    unnamed x15 -> x17, local copies, waits for them, and re-layouts: 3.22 us -> 5.21 us
    reshape x4, local copies, waits for them, and re-layouts: 2.92 us -> 1.37 us  [the longest x2 0.69 us: fused(): mask.reshape(own_templates, picks * channels)]
where the time goes in v6:
time: 88.3 us; the launch traced here: 87.9 us
  Pallas kernels  78.6 us (89%)
  local copies, waits for them, and re-layouts  8.34 us (9%)
    pallas_call x1, Pallas kernels, fused(): pl.pallas_call(functools.partial(fused_kernel, picks, channels, pieces),...  78.6 us
    unnamed x17, local copies, waits for them, and re-layouts  5.21 us

profile of v6, /device:TPU:0, one launch (start us, length us, event | category | flops | bytes accessed | tf_op | source)
XLA Modules:
  0.0 87.9 jit_solution(15348029008094230752)
XLA Ops:
  0.0 1.1 %copy.24 = bf16[24,10,3,200]{3,1,0,2:T(8,128)(2,1)S(1)} copy(bf16[24,10,3,200]{3,0,2,1:T(8,128)(2,1)} %param.7) | data formatting | bytes 576000 | tf_op args[1]
  1.1 0.0 copy-start.1
  1.1 0.9 %pad.8.shapes_ref = bf16[3,24,16,256]{3,2,1,0:T(8,128)(2,1)} pad(bf16[3,24,10,200]{3,2,1,0:T(8,128)(2,1)S(1)} %bitcast.15, bf16[]{:T(256)} %constant.8.clone.1), padding=0_0x0_0x0_6x0_56 | pad | bytes 877826 | tf_op jit(solution)/shard_map/jit(_pad)/pad | solution.py:298
  2.0 0.0 copy-done.1
  2.1 0.1 reshape.18
  2.2 0.0 copy-start
  2.2 0.7 pad.9.mine_ref
  2.9 0.7 fusion.3.band_ref
  3.6 0.0 copy-done
  3.6 0.2 multiply_reduce_fusion
  3.8 0.0 copy-start.2
  3.8 0.7 copy.18.power
  4.5 0.0 copy-done.2
  4.5 0.0 copy-start.3
  4.5 0.7 copy.19.mask
  5.2 0.0 copy-done.3
  5.2 0.0 copy-start.4
  5.2 0.7 copy.15.owner
  5.9 0.0 copy-done.4
  5.9 0.7 copy.16.place
  6.6 0.0 copy-done.5
  6.6 0.7 copy.17.shift
  7.3 78.6 %shard_map.64 = f32[24,32,128]{2,1,0:T(8,128)} custom-call(s32[24,10]{1,0:T(8,128)} %copy.15.owner, s32[24,10]{1,0:T(8,128)} %copy.16.place, s32[24,10]{1,0:T(8,128)} %copy.17.shift, f32[24,30]{1,0:T(8,128)} %copy.18.power, f32[24,30]{1,0:T(8,128)} %copy.19.mask, bf16[384,128]{1,0:T(8,128)(2,1)} %fusion.3.band_ref, bf16[3,24,16,256]{3,2,1,0:T(8,128)(2,1)} %pad.8.shapes_ref, ...), custom_call_target="tpu_custom_call" | custom-call | tf_op jit(solution)/shard_map/pallas_call | solution.py:304
  85.9 2.0 %copy.25 = f32[3,8,32,128]{3,1,2,0:T(8,128)} copy(f32[3,8,32,128]{3,2,1,0:T(8,128)} %bitcast.16) | data formatting | bytes 786432
  (5 shorter events, 0.1 us)
Async XLA Ops:
  1.1 0.9 %copy-start.1 = (bf16[8,3,4480]{2,0,1:T(8,128)(2,1)S(1)}, bf16[8,3,4480]{2,0,1:T(8,128)(2,1)}, u32[]{:S(2)}) copy-start(bf16[8,3,4480]{2,0,1:T(8,128)(2,1)} %param.6) | copy-start | bytes 645124
  2.2 1.4 %copy-start = (bf16[24,10,3,200]{3,0,2,1:T(8,128)(2,1)S(1)}, bf16[24,10,3,200]{3,0,2,1:T(8,128)(2,1)}, u32[]{:S(2)}) copy-start(bf16[24,10,3,200]{3,0,2,1:T(8,128)(2,1)} %param.7) | copy-start | bytes 864004
  3.8 0.7 copy-start.2
  4.5 0.7 copy-start.3
  5.2 0.7 copy-start.4
  5.9 0.7 copy-start.5
